TPU v7x, 1024 devices: a whole 8x8x8 slice. The times are simulated.
1024 devices in a mesh: expert: 64 (over z, x), dp: 16 (over y, core).
Axes of the slice: x: 8, y: 8, z: 8, core: 2. Of those that a mesh axis runs over, the one named last changes fastest.
Arguments:
- tokens: bfloat16 [8192, 7168], P('expert', 'dp'), may hold values from -6 to 6
- routes: int32 [8192, 1], P('expert'), may hold values from 0 to 15; in each aligned block of 128 rows (0 to 127, 128 to 255, ...) at most 10 rows name the same one
- route_weight: bfloat16 [8192, 1], P('expert'), may hold values from 0.099609375 to 1
- out_grad: bfloat16 [8192, 7168], P('expert', 'dp'), may hold values from -0.29882812 to 0.29882812
- w_gate: bfloat16 [7168, 32768], P('dp', 'expert'), may hold values from -0.0625 to 0.0625
- w_up: bfloat16 [7168, 32768], P('dp', 'expert'), may hold values from -0.0625 to 0.0625
- w_down: bfloat16 [32768, 7168], P('expert', 'dp'), may hold values from -0.125 to 0.125
Outputs:
- grad_gate: bfloat16 [7168, 32768], P('dp', 'expert')
- grad_up: bfloat16 [7168, 32768], P('dp', 'expert')
Inputs may be any that keep to these rules, and one draw needn't show every extreme that they name: In each aligned block of 128 tokens, the tokens of one index of expert, no expert is named by more than 10 routes, and in every draw some block has an expert named by exactly 10. A token's routes name different experts.
All inputs are finite; a program needn't handle non-finite values.
Results may differ from a plain program's by a relative error of at most 0.035.
Values may be sent and summed in bfloat16 or wider, within the bound.
No kernel may reach another device: no remote copies, remote signals or barrier semaphores. Data moves between devices by JAX's collectives and lax.ppermute only.
A program may use at most 32 MiB of HBM per device.

v0:
```python
import jax
import jax.numpy as jnp
from jax import lax
from jax.sharding import PartitionSpec as P

SLICES = 4


def activate(totals, hidden):
    gate_pre = totals[:, :hidden]
    up_pre = totals[:, hidden : 2 * hidden]
    act_grad = totals[:, 2 * hidden :]
    sigmoid = jax.nn.sigmoid(gate_pre)
    gate_grad = (act_grad * up_pre * sigmoid * (1.0 + gate_pre * (1.0 - sigmoid))).astype(
        jnp.bfloat16
    )
    up_grad = (act_grad * gate_pre * sigmoid).astype(jnp.bfloat16)
    return jnp.concatenate([gate_grad, up_grad], axis=1)


def shards(tokens, routes, route_weight, out_grad, w_gate, w_up, w_down):
    columns = lax.axis_size("expert")
    experts_here = columns // SLICES
    tok_count, width_part = tokens.shape
    routes_each = routes.shape[1]
    hidden = w_gate.shape[1]
    capacity = max(2, tok_count * routes_each * 5 // (experts_here * 4))
    entries = routes.reshape(-1)
    onehot = (entries[:, None] == jnp.arange(experts_here, dtype=jnp.int32)[None, :]).astype(
        jnp.int32
    )
    before = jnp.cumsum(onehot, axis=0) - onehot
    slot_of = jnp.sum(onehot * before, axis=1)
    key_slot = entries * capacity + slot_of
    placed = (
        key_slot[None, :] == jnp.arange(experts_here * capacity, dtype=jnp.int32)[:, None]
    ).astype(jnp.float32)
    placed = placed.reshape(experts_here * capacity, tok_count, routes_each)
    select_rows = jnp.sum(placed, axis=2).astype(jnp.bfloat16)
    scaled = jnp.sum(placed * route_weight.astype(jnp.float32)[None, :, :], axis=2).astype(
        jnp.bfloat16
    )
    token_buffer = jnp.dot(select_rows, tokens, preferred_element_type=jnp.float32).astype(
        jnp.bfloat16
    )
    cotan_buffer = jnp.dot(scaled, out_grad, preferred_element_type=jnp.float32).astype(
        jnp.bfloat16
    )
    payload = jnp.concatenate([token_buffer, cotan_buffer], axis=1).reshape(
        experts_here, capacity, 2 * width_part
    )
    spread = jnp.repeat(payload, SLICES, axis=0)
    arrived = lax.all_to_all(spread, "expert", split_axis=0, concat_axis=0, tiled=True).reshape(
        -1, 2 * width_part
    )
    token_rows = arrived[:, :width_part]
    cotan_rows = arrived[:, width_part:]
    partials = jnp.concatenate(
        [
            jnp.dot(token_rows, w_gate, preferred_element_type=jnp.float32),
            jnp.dot(token_rows, w_up, preferred_element_type=jnp.float32),
            lax.dot_general(
                cotan_rows, w_down, (((1,), (1,)), ((), ())), preferred_element_type=jnp.float32
            ),
        ],
        axis=1,
    )
    rounded = lax.optimization_barrier(partials.astype(jnp.bfloat16)).astype(jnp.float32)
    factors = activate(lax.psum(rounded.astype(jnp.bfloat16), "dp").astype(jnp.float32), hidden)
    weight_grads = lax.dot_general(
        token_rows, factors, (((0,), (0,)), ((), ())), preferred_element_type=jnp.float32
    )
    return (
        weight_grads[:, :hidden].astype(jnp.bfloat16),
        weight_grads[:, hidden:].astype(jnp.bfloat16),
    )


def solution(mesh):
    in_specs = (
        P("expert", "dp"),
        P("expert", None),
        P("expert", None),
        P("expert", "dp"),
        P("dp", "expert"),
        P("dp", "expert"),
        P("expert", "dp"),
    )
    out_specs = (P("dp", "expert"), P("dp", "expert"))
    return jax.shard_map(shards, mesh=mesh, in_specs=in_specs, out_specs=out_specs, check_vma=False)
```

profile of v0, /device:TPU:1, one launch (start us, length us, event | category | flops | bytes accessed | tf_op | source)
XLA Modules:
  0.0 220.1 jit_solution(11035118478974143003)
XLA Ops:
  7.2 0.0 copy-start
  7.2 0.0 all-reduce.2.cloned.1.call-start
  7.2 0.8 fusion.10
  8.0 0.2 reduce_window_sum.11
  8.2 0.8 select_reduce_fusion
  9.0 0.7 multiply_add_fusion
  9.7 1.1 convolution_convert_fusion.5
  10.8 1.1 convolution_convert_fusion.4
  11.9 0.1 pad_maximum_fusion.1
  12.0 0.1 reshape.63
  12.1 0.1 broadcast_in_dim.2
  12.3 67.4 %all_to_all.5 = bf16[64,10,896]{2,1,0:T(8,128)(2,1)S(1)} all-to-all(bf16[64,10,896]{2,1,0:T(8,128)(2,1)S(1)} %bitcast.12), channel_id=1, replica_groups=mesh['expert'=64,'dp'=16] {'expert'}, dimensions={0} | all-to-all | bytes 2293760 | tf_op jit(solution)/shard_map/all_to_all | solution.py:53
  79.7 0.4 reshape.65
  80.1 0.0 copy-done
  80.1 0.0 copy-start.1
  80.2 0.6 convolution_convert_fusion.2
  80.8 0.4 copy-done.1
  81.2 0.0 copy-start.2
  81.2 0.7 convolution_convert_fusion.1
  81.9 0.3 copy-done.2
  82.2 0.6 convolution_convert_fusion.3
  82.8 1.4 pad_maximum_fusion
  84.3 0.0 all-reduce.2.cloned.1.call-update
  84.3 124.6 %all-reduce.2.cloned.1.call-done = bf16[640,1536]{0,1:T(8,128)(2,1)} async-done(((bf16[640,1536]{0,1:T(8,128)(2,1)}), bf16[640,1536]{0,1:T(8,128)(2,1)}) %all-reduce.2.cloned.1.call-update) | async-done | bytes 1966096 | tf_op jit(solution)/shard_map/psum | solution.py:69
  208.9 1.8 convert_element_type.43
  210.7 0.6 fusion.2
  211.3 1.0 convolution_convert_fusion
  212.3 1.0 fusion.17
Async XLA Ops:
  7.2 73.0 %copy-start = (bf16[448,512]{1,0:T(8,128)(2,1)S(1)}, bf16[448,512]{1,0:T(8,128)(2,1)}, u32[]{:S(2)}) copy-start(bf16[448,512]{1,0:T(8,128)(2,1)} %param.12) | copy-start | bytes 1376260
  7.2 201.7 %all-reduce.2.cloned.1.call-start = ((), (), s32[]{:S(2)}) async-start(), calls=%async_computation.1 | async-start | bytes 3932160 | tf_op jit(solution)/shard_map/psum | solution.py:69
  80.1 1.0 copy-start.1
  81.2 1.0 copy-start.2
Sparse Core Ops, SparseCore 0:
  84.4 124.4 all-reduce.1
where the time goes:
time: 220 us
  waiting for transfers between devices  125 us (57%)
  blocking collectives  67.4 us (31%)
  between operations  14.1 us (6%)
  other arithmetic  6.44 us (3%)
  matrix products  5.2 us (2%)
  local copies, waits for them, and re-layouts  2.29 us (1%)
    psum x1, waiting for transfers between devices, shards(): lax.psum(rounded.astype(jnp.bfloat16), 'dp').astype(jnp.float32)  125 us
    all_to_all x1, blocking collectives, shards(): lax.all_to_all(spread, 'expert', split_axis=0, concat_axis=0, tiled=True)  67.4 us
  transfers between devices with their start and end apart: 1, of which 1 were waited for; matrix products, arithmetic and copies ran while one was open for 0% of the time, Pallas kernels for 0%

commit v1 on v0

v1 whole, which is shorter than its diff:
```python
import jax
import jax.numpy as jnp
from jax import lax
from jax.experimental import pallas as pl
from jax.experimental.pallas import tpu as pltpu
from jax.sharding import Mesh, PartitionSpec as P

SLICES = 4
CORES = 2
LANES = 128
MAIN = 8
VMEM = pltpu.VMEM
F32 = jnp.float32
BF16 = jnp.bfloat16


def whole(count):
    return [pl.BlockSpec(memory_space=VMEM)] * count


def pack_kernel(capacity, routes_ref, weight_ref, tokens_ref, grad_ref, out_ref, rows_ref):
    width, count = tokens_ref.shape
    experts = out_ref.shape[0] // SLICES
    chunks = 2 * width // LANES
    extra = capacity - MAIN
    tail_rows = out_ref.shape[1] - chunks * MAIN
    rows_ref[:width] = (weight_ref[...].astype(F32) * grad_ref[...].astype(F32)).astype(BF16)
    rows_ref[width:] = tokens_ref[...]
    expert = routes_ref[...]
    onehot = (expert == lax.broadcasted_iota(jnp.int32, (experts, count), 0)).astype(F32)
    earlier = lax.broadcasted_iota(jnp.int32, (count, count), 0)
    later = lax.broadcasted_iota(jnp.int32, (count, count), 1)
    before = jnp.dot(onehot, (earlier < later).astype(F32), preferred_element_type=F32)
    slot = jnp.sum(onehot * before, axis=0, keepdims=True).astype(jnp.int32)
    contract = (((1,), (1,)), ((), ()))
    place = lax.broadcasted_iota(jnp.int32, (experts * MAIN, count), 0)
    main_pick = ((slot < MAIN) & (expert * MAIN + slot == place)).astype(F32).astype(BF16)
    main = lax.dot_general(main_pick, rows_ref[...], contract, preferred_element_type=F32)
    place = lax.broadcasted_iota(jnp.int32, (experts * tail_rows, count), 0)
    tail = jnp.zeros((experts * tail_rows, LANES), F32)
    for c in range(chunks):
        target = expert * tail_rows + c * extra + slot - MAIN
        pick = ((slot >= MAIN) & (target == place)).astype(F32).astype(BF16)
        tail = tail + lax.dot_general(
            pick, rows_ref[c * LANES : (c + 1) * LANES], contract, preferred_element_type=F32
        )
    for e in range(experts):
        pieces = [
            main[e * MAIN : (e + 1) * MAIN, c * LANES : (c + 1) * LANES] for c in range(chunks)
        ]
        pieces.append(tail[e * tail_rows : (e + 1) * tail_rows])
        block = jnp.concatenate(pieces, axis=0).astype(BF16)
        for copy in range(SLICES):
            out_ref[e * SLICES + copy] = block


def partial_kernel(
    capacity, step, core_ref, arrived_ref, gate_ref, up_ref, down_ref,
    rows_ref, send_ref, keep_ref, gate_up_ref, down_pad_ref,
):
    sources, block_rows, _ = arrived_ref.shape
    slots, width = rows_ref.shape
    half = slots // CORES
    chunks = width // LANES
    depth, hidden = gate_ref.shape
    wide = gate_up_ref.shape[0]
    extra = capacity - MAIN
    tail_rows = block_rows - chunks * MAIN
    gate_up_ref[: wide - depth] = jnp.zeros((wide - depth, 2 * hidden), BF16)
    gate_up_ref[wide - depth :, :hidden] = gate_ref[...]
    gate_up_ref[wide - depth :, hidden:] = up_ref[...]
    down_pad_ref[depth:] = jnp.zeros((wide - depth, hidden), BF16)
    down_pad_ref[:depth] = down_ref[...]

    def unpack(pair, carry):
        first = arrived_ref[2 * pair][: chunks * MAIN].astype(F32)
        second = arrived_ref[2 * pair + 1][: chunks * MAIN].astype(F32)
        at = pl.multiple_of(pair * 2 * MAIN, 2 * MAIN)
        for c in range(chunks):
            both = jnp.concatenate(
                [first[c * MAIN : (c + 1) * MAIN], second[c * MAIN : (c + 1) * MAIN]], axis=0
            )
            rows_ref[pl.ds(at, 2 * MAIN), c * LANES : (c + 1) * LANES] = both.astype(BF16)
        return carry

    lax.fori_loop(0, sources // 2, unpack, 0, unroll=4)
    group = 16
    place = lax.broadcasted_iota(jnp.int32, (chunks * group * extra, group * tail_rows), 0)
    origin = lax.broadcasted_iota(jnp.int32, (chunks * group * extra, group * tail_rows), 1)
    chunk = place // (group * extra)
    inside = place % (group * extra)
    wanted = (inside // extra) * tail_rows + chunk * extra + inside % extra
    pick = (wanted == origin).astype(F32).astype(BF16)
    for g in range(sources // group):
        tails = [
            arrived_ref[g * group + s].astype(F32)[chunks * MAIN :] for s in range(group)
        ]
        tail = jnp.concatenate(tails, axis=0).astype(BF16)
        moved = jnp.dot(pick, tail, preferred_element_type=F32).astype(BF16)
        at = sources * MAIN + g * group * extra
        for c in range(chunks):
            rows_ref[at : at + group * extra, c * LANES : (c + 1) * LANES] = moved[
                c * group * extra : (c + 1) * group * extra
            ]

    core = core_ref[0]

    def multiply(start, out_ref):
        for i in range(half // step):
            at = pl.multiple_of(start + i * step, 16)
            token_part = rows_ref[pl.ds(at, step), width - wide :]
            cotan_part = rows_ref[pl.ds(at, step), :wide]
            here = slice(i * step, (i + 1) * step)
            out_ref[here, : 2 * hidden] = jnp.dot(
                token_part, gate_up_ref[...], preferred_element_type=F32
            ).astype(BF16)
            out_ref[here, 2 * hidden :] = jnp.dot(
                cotan_part, down_pad_ref[...], preferred_element_type=F32
            ).astype(BF16)

    multiply((1 - core) * half, send_ref)
    multiply(core * half, keep_ref)


def factor_kernel(parts_ref, out_ref):
    parts, _, columns = parts_ref.shape
    hidden = columns // 3
    total = parts_ref[0].astype(F32)
    for j in range(1, parts):
        total = total + parts_ref[j].astype(F32)
    gate_pre = total[:, :hidden]
    up_pre = total[:, hidden : 2 * hidden]
    act_grad = total[:, 2 * hidden :]
    sigmoid = 1.0 / (1.0 + jnp.exp(-gate_pre))
    gate_grad = (act_grad * up_pre * sigmoid * (1.0 + gate_pre * (1.0 - sigmoid))).astype(BF16)
    up_grad = (act_grad * gate_pre * sigmoid).astype(BF16)
    for j in range(out_ref.shape[0]):
        out_ref[j, :, :hidden] = gate_grad
        out_ref[j, :, hidden:] = up_grad


def weight_kernel(core_ref, rows_ref, own_ref, other_ref, gate_ref, up_ref):
    slots, width = rows_ref.shape
    depth, hidden = gate_ref.shape
    half = slots // CORES
    wide = -(-depth // LANES) * LANES
    core = core_ref[0]
    own_at = pl.multiple_of(core * half, 16)
    other_at = pl.multiple_of((1 - core) * half, 16)
    own_rows = rows_ref[pl.ds(own_at, half), width - wide :]
    other_rows = rows_ref[pl.ds(other_at, half), width - wide :]
    contract = (((0,), (0,)), ((), ()))
    for out_ref, left in ((gate_ref, 0), (up_ref, hidden)):
        block = slice(left, left + hidden)
        total = lax.dot_general(own_rows, own_ref[:, block], contract, preferred_element_type=F32)
        total = total + lax.dot_general(
            other_rows, other_ref[:, block], contract, preferred_element_type=F32
        )
        out_ref[...] = total[wide - depth :].astype(BF16)


def shards(tokens, routes, route_weight, out_grad, w_gate, w_up, w_down):
    columns = lax.axis_size("expert")
    chips = lax.axis_size("chip")
    experts = columns // SLICES
    count, depth = tokens.shape
    hidden = w_gate.shape[1]
    width = 2 * depth
    chunks = width // LANES
    capacity = max(2, count * 5 // (experts * 4))
    slots = columns * capacity
    half = slots // CORES
    block_rows = chunks * MAIN + -(-chunks * (capacity - MAIN) // 8) * 8
    wide = -(-depth // LANES) * LANES
    core = lax.axis_index("core").astype(jnp.int32).reshape(1)
    pairs = [(c, (c + 1) % CORES) for c in range(CORES)]
    smem = pl.BlockSpec(memory_space=pltpu.SMEM)

    blocks = pl.pallas_call(
        lambda *refs: pack_kernel(capacity, *refs),
        out_shape=jax.ShapeDtypeStruct((columns, block_rows, LANES), BF16),
        in_specs=whole(4),
        out_specs=whole(1)[0],
        scratch_shapes=[VMEM((width, count), BF16)],
        compiler_params=pltpu.CompilerParams(vmem_limit_bytes=16 << 20),
        name="pack",
    )(routes.T, route_weight.T, tokens.T, out_grad.T)
    arrived = lax.all_to_all(blocks, "expert", split_axis=0, concat_axis=0, tiled=True)
    rows, send, keep = pl.pallas_call(
        lambda *refs: partial_kernel(capacity, 80, *refs),
        out_shape=(
            jax.ShapeDtypeStruct((slots, width), BF16),
            jax.ShapeDtypeStruct((half, 3 * hidden), BF16),
            jax.ShapeDtypeStruct((half, 3 * hidden), BF16),
        ),
        in_specs=[smem] + whole(4),
        out_specs=tuple(whole(3)),
        scratch_shapes=[VMEM((wide, 2 * hidden), BF16), VMEM((wide, hidden), BF16)],
        compiler_params=pltpu.CompilerParams(vmem_limit_bytes=24 << 20),
        name="partial",
    )(core, arrived, w_gate, w_up, w_down.T)
    sibling = lax.ppermute(send, "core", pairs)
    summed = (keep.astype(F32) + sibling.astype(F32)).astype(BF16)
    parts = lax.all_to_all(
        summed.reshape(chips, half // chips, 3 * hidden),
        "chip", split_axis=0, concat_axis=0, tiled=True,
    )
    spread = pl.pallas_call(
        factor_kernel,
        out_shape=jax.ShapeDtypeStruct((chips, half // chips, 2 * hidden), BF16),
        in_specs=whole(1),
        out_specs=whole(1)[0],
        compiler_params=pltpu.CompilerParams(vmem_limit_bytes=16 << 20),
        name="factor",
    )(parts)
    own = lax.all_to_all(
        spread, "chip", split_axis=0, concat_axis=0, tiled=True
    ).reshape(half, 2 * hidden)
    other = lax.ppermute(own, "core", pairs)
    return pl.pallas_call(
        weight_kernel,
        out_shape=(
            jax.ShapeDtypeStruct((depth, hidden), BF16),
            jax.ShapeDtypeStruct((depth, hidden), BF16),
        ),
        in_specs=[smem] + whole(3),
        out_specs=tuple(whole(2)),
        compiler_params=pltpu.CompilerParams(vmem_limit_bytes=24 << 20),
        name="weight",
    )(core, rows, own, other)


def solution(mesh):
    devices = mesh.devices
    columns, members = devices.shape
    split = Mesh(devices.reshape(columns, members // CORES, CORES), ("expert", "chip", "core"))
    width = ("chip", "core")
    in_specs = (
        P("expert", width),
        P("expert", None),
        P("expert", None),
        P("expert", width),
        P(width, "expert"),
        P(width, "expert"),
        P("expert", width),
    )
    out_specs = (P(width, "expert"), P(width, "expert"))
    return jax.shard_map(shards, mesh=split, in_specs=in_specs, out_specs=out_specs, check_vma=False)
```

time: 220 us -> 133 us (0.60)
  waiting for transfers between devices: 125 us -> 33.8 us
  starting transfers between devices: 0.04 us -> 34.1 us
  blocking collectives: 67.4 us -> 53.9 us
  between operations: 14.1 us -> 0.69 us
  Pallas kernels: 0 us -> 6.63 us
  other arithmetic: 6.44 us -> 0.29 us
  matrix products: 5.2 us -> 0 us
    psum x1 -> x0, waiting for transfers between devices: 125 us -> none  [shards(): lax.psum(rounded.astype(jnp.bfloat16), 'dp').astype(jnp.float32)]
    all_to_all x0 -> x1, waiting for transfers between devices: none -> 29.9 us  [shards(): lax.all_to_all(blocks, 'expert', split_axis=0, concat_axis=0, tiled=True)]
    all_to_all x0 -> x1, starting transfers between devices: none -> 23.3 us  [shards(): lax.all_to_all(blocks, 'expert', split_axis=0, concat_axis=0, tiled=True)]
    all_to_all x1 -> x2, blocking collectives: 67.4 us -> 53.9 us  [the longest x1 33.6 us: shards(): lax.all_to_all(summed.reshape(chips, half // chips, 3 * hidden), 'chip',...]
    ppermute x0 -> x2, starting transfers between devices: none -> 10.8 us  [the longest x1 5.58 us: shards(): sibling = lax.ppermute(send, 'core', pairs)]
    pallas_call x0 -> x4, Pallas kernels: none -> 6.63 us  [the longest x1 2.9 us: shards(): pl.pallas_call(lambda *refs: partial_kernel(capacity, 80, *refs), out_sha...]
    dot_general x6 -> x0, matrix products: 5.2 us -> none  [the longest x1 1.12 us: shards(): jnp.dot(scaled, out_grad, preferred_element_type=jnp.float32)]
    ppermute x0 -> x2, waiting for transfers between devices: none -> 3.87 us  [the longest x1 2.17 us: shards(): sibling = lax.ppermute(send, 'core', pairs)]
  transfers between devices with their start and end apart: 1 -> 3, of which waited for: 1 -> 3; matrix products, arithmetic and copies ran while one was open for 0% -> 0% of each run, Pallas kernels for 0% -> 0%
where the time goes in v1:
time: 133 us; the launch traced here: 132 us
  blocking collectives  53.9 us (41%)
  starting transfers between devices  34.1 us (26%)
  waiting for transfers between devices  33.8 us (25%)
  Pallas kernels  6.63 us (5%)
  local copies, waits for them, and re-layouts  3.11 us (2%)
    all_to_all x1, blocking collectives, shards(): lax.all_to_all(summed.reshape(chips, half // chips, 3 * hidden), 'chip',...  33.6 us
    all_to_all x1, waiting for transfers between devices, shards(): lax.all_to_all(blocks, 'expert', split_axis=0, concat_axis=0, tiled=True)  29.9 us
    all_to_all x1, starting transfers between devices, shards(): lax.all_to_all(blocks, 'expert', split_axis=0, concat_axis=0, tiled=True)  23.3 us
    all_to_all x1, blocking collectives, shards(): lax.all_to_all(spread, 'chip', split_axis=0, concat_axis=0, tiled=True)  20.3 us
    ppermute x1, starting transfers between devices, shards(): sibling = lax.ppermute(send, 'core', pairs)  5.58 us
    ppermute x1, starting transfers between devices, shards(): other = lax.ppermute(own, 'core', pairs)  5.21 us
    unnamed x14, local copies, waits for them, and re-layouts  3.11 us
    pallas_call x1, Pallas kernels, shards(): pl.pallas_call(lambda *refs: partial_kernel(capacity, 80, *refs), out_sha...  2.9 us
  transfers between devices with their start and end apart: 3, of which 3 were waited for; matrix products, arithmetic and copies ran while one was open for 0% of the time, Pallas kernels for 0%

profile of v1, /device:TPU:1, one launch (start us, length us, event | category | flops | bytes accessed | tf_op | source)
XLA Modules:
  0.0 132.5 jit_solution(3113383493294642446)
XLA Ops:
  0.6 0.0 copy-start.3
  0.6 0.9 copy-done.3
  1.5 0.0 copy-start.4
  1.5 0.9 copy-done.4
  2.4 0.0 copy-start.5
  2.4 0.7 copy-done.5
  3.1 0.0 copy-start.6
  3.1 0.7 copy-done.6
  3.7 1.5 %pack.1 = bf16[64,72,128]{2,1,0:T(8,128)(2,1)} custom-call(s32[1,128]{1,0:T(1,128)S(1)} %bitcast.13, bf16[1,128]{1,0:T(2,128)(2,1)S(1)} %bitcast.14, bf16[448,128]{1,0:T(8,128)(2,1)S(1)} %bitcast.11, bf16[448,128]{1,0:T(8,128)(2,1)S(1)} %bitcast.12), custom_call_target="tpu_custom_call" | custom-call | tf_op jit(solution)/shard_map/pack/pallas_call | solution.py:179
  5.2 0.0 copy-start
  5.3 0.0 copy-start.1
  5.3 0.0 copy-start.2
  5.3 23.3 %all-to-all-start = ((bf16[64,72,128]{2,1,0:T(8,128)(2,1)}), bf16[64,72,128]{2,1,0:T(8,128)(2,1)S(1)}, u32[]{:S(2)}, u32[]{:S(2)}) async-start(bf16[64,72,128]{2,1,0:T(8,128)(2,1)} %pack.1), calls=%async_computation | async-start | bytes 2359296 | tf_op jit(solution)/shard_map/all_to_all | solution.py:188
  28.6 29.9 %all-to-all-done.refs_1_ = bf16[64,72,128]{2,1,0:T(8,128)(2,1)S(1)} async-done(((bf16[64,72,128]{2,1,0:T(8,128)(2,1)}), bf16[64,72,128]{2,1,0:T(8,128)(2,1)S(1)}, u32[]{:S(2)}, u32[]{:S(2)}) %all-to-all-start) | async-done | bytes 1179680 | tf_op jit(solution)/shard_map/all_to_all | solution.py:188
  58.5 0.0 copy-done
  58.5 0.0 copy-done.1
  58.5 0.0 copy-done.2
  58.5 2.9 %partial.1 = (bf16[640,896]{1,0:T(8,128)(2,1)S(1)}, bf16[320,1536]{1,0:T(8,128)(2,1)S(1)}, bf16[320,1536]{1,0:T(8,128)(2,1)S(1)}) custom-call(s32[1]{0:T(128)} %bitcast.refs_0_.core_ref, bf16[64,72,128]{2,1,0:T(8,128)(2,1)S(1)} %all-to-all-done.refs_1_, bf16[448,512]{1,0:T(8,128)(2,1)S(1)} %copy-done, bf16[448,512]{1,0:T(8,128)(2,1)S(1)} %copy-done.1, ...), custom_call_target="tpu_custom_call" | custom-call | tf_op jit(solution)/shard_map/partial/pallas_call | solution.py:189
  61.4 5.6 %collective-permute-start = (bf16[320,1536]{1,0:T(8,128)(2,1)S(1)}, bf16[320,1536]{1,0:T(8,128)(2,1)S(1)}, u32[]{:S(2)}, u32[]{:S(2)}) collective-permute-start(bf16[320,1536]{1,0:T(8,128)(2,1)S(1)} %get-tuple-element.7), channel_id=1, source_target_pairs={{0,1},{1,0},{2,3},{3,2},{4,5},{5,4},{6,7},{7,6},{8,9},{9,8},{10,11... | collective-permute-start | bytes 2949128 | tf_op jit(solution)/shard_map/ppermute | solution.py:202
  67.0 2.2 %collective-permute-done = bf16[320,1536]{1,0:T(8,128)(2,1)S(1)} collective-permute-done((bf16[320,1536]{1,0:T(8,128)(2,1)S(1)}, bf16[320,1536]{1,0:T(8,128)(2,1)S(1)}, u32[]{:S(2)}, u32[]{:S(2)}) %collective-permute-start) | collective-permute-done | bytes 983072 | tf_op jit(solution)/shard_map/ppermute | solution.py:202
  69.1 0.3 add_convert_fusion
  69.4 33.6 %all_to_all.15.parts_ref = bf16[8,40,1536]{2,1,0:T(8,128)(2,1)S(1)} all-to-all(bf16[8,40,1536]{2,1,0:T(8,128)(2,1)S(1)} %bitcast.15), channel_id=1, replica_groups=mesh['expert'=64,'chip'=8,'core'=2] {'chip'}, dimensions={0} | all-to-all | bytes 1966080 | tf_op jit(solution)/shard_map/all_to_all | solution.py:204
  103.0 0.2 factor.1
  103.2 20.3 %all_to_all.16 = bf16[8,40,1024]{2,1,0:T(8,128)(2,1)S(1)} all-to-all(bf16[8,40,1024]{2,1,0:T(8,128)(2,1)S(1)} %factor.1), channel_id=1, replica_groups=mesh['expert'=64,'chip'=8,'core'=2] {'chip'}, dimensions={0} | all-to-all | bytes 1310720 | tf_op jit(solution)/shard_map/all_to_all | solution.py:216
  123.5 5.2 %collective-permute-start.1 = (bf16[320,1024]{1,0:T(8,128)(2,1)S(1)}, bf16[320,1024]{1,0:T(8,128)(2,1)S(1)}, u32[]{:S(2)}, u32[]{:S(2)}) collective-permute-start(bf16[320,1024]{1,0:T(8,128)(2,1)S(1)} %bitcast.8), channel_id=1, source_target_pairs={{0,1},{1,0},{2,3},{3,2},{4,5},{5,4},{6,7},{7,6},{8,9},{9,8},{10,11... | collective-permute-start | bytes 1966088 | tf_op jit(solution)/shard_map/ppermute | solution.py:219
  128.7 1.7 %collective-permute-done.1.other_ref = bf16[320,1024]{1,0:T(8,128)(2,1)S(1)} collective-permute-done((bf16[320,1024]{1,0:T(8,128)(2,1)S(1)}, bf16[320,1024]{1,0:T(8,128)(2,1)S(1)}, u32[]{:S(2)}, u32[]{:S(2)}) %collective-permute-start.1) | collective-permute-done | bytes 655392 | tf_op jit(solution)/shard_map/ppermute | solution.py:219
  130.4 2.1 %weight.1 = (bf16[448,512]{1,0:T(8,128)(2,1)}, bf16[448,512]{1,0:T(8,128)(2,1)}) custom-call(s32[1]{0:T(128)} %bitcast.refs_0_.core_ref, bf16[640,896]{1,0:T(8,128)(2,1)S(1)} %get-tuple-element.5.rows_ref, bf16[320,1024]{1,0:T(8,128)(2,1)S(1)} %bitcast.9, bf16[320,1024]{1,0:T(8,128)(2,1)S(1)} %collective-permute-done.1.other_ref), custom_call_target="tpu_custom_call" | custom-call | tf_op jit(solution)/shard_map/weight/pallas_call | solution.py:220
Async XLA Ops:
  0.6 0.9 copy-start.3
  1.5 0.9 copy-start.4
  2.4 0.7 copy-start.5
  3.1 0.7 copy-start.6
  5.2 53.2 %copy-start = (bf16[448,512]{1,0:T(8,128)(2,1)S(1)}, bf16[448,512]{1,0:T(8,128)(2,1)}, u32[]{:S(2)}) copy-start(bf16[448,512]{1,0:T(8,128)(2,1)} %refs_2_.1) | copy-start | bytes 1376260
  5.3 53.2 %copy-start.1 = (bf16[448,512]{1,0:T(8,128)(2,1)S(1)}, bf16[448,512]{1,0:T(8,128)(2,1)}, u32[]{:S(2)}) copy-start(bf16[448,512]{1,0:T(8,128)(2,1)} %refs_3_.1) | copy-start | bytes 1376260
  5.3 53.2 %copy-start.2 = (bf16[512,448]{0,1:T(8,128)(2,1)S(1)}, bf16[512,448]{0,1:T(8,128)(2,1)}, u32[]{:S(2)}) copy-start(bf16[512,448]{0,1:T(8,128)(2,1)} %param.13) | copy-start | bytes 1376260
  5.3 53.2 %all-to-all-start = ((bf16[64,72,128]{2,1,0:T(8,128)(2,1)}), bf16[64,72,128]{2,1,0:T(8,128)(2,1)S(1)}, u32[]{:S(2)}, u32[]{:S(2)}) async-start(bf16[64,72,128]{2,1,0:T(8,128)(2,1)} %pack.1), calls=%async_computation | async-start | bytes 2359296 | tf_op jit(solution)/shard_map/all_to_all | solution.py:188
  61.4 7.8 %collective-permute-start = (bf16[320,1536]{1,0:T(8,128)(2,1)S(1)}, bf16[320,1536]{1,0:T(8,128)(2,1)S(1)}, u32[]{:S(2)}, u32[]{:S(2)}) collective-permute-start(bf16[320,1536]{1,0:T(8,128)(2,1)S(1)} %get-tuple-element.7), channel_id=1, source_target_pairs={{0,1},{1,0},{2,3},{3,2},{4,5},{5,4},{6,7},{7,6},{8,9},{9,8},{10,11... | collective-permute-start | bytes 2949128 | tf_op jit(solution)/shard_map/ppermute | solution.py:202
  123.5 6.9 %collective-permute-start.1 = (bf16[320,1024]{1,0:T(8,128)(2,1)S(1)}, bf16[320,1024]{1,0:T(8,128)(2,1)S(1)}, u32[]{:S(2)}, u32[]{:S(2)}) collective-permute-start(bf16[320,1024]{1,0:T(8,128)(2,1)S(1)} %bitcast.8), channel_id=1, source_target_pairs={{0,1},{1,0},{2,3},{3,2},{4,5},{5,4},{6,7},{7,6},{8,9},{9,8},{10,11... | collective-permute-start | bytes 1966088 | tf_op jit(solution)/shard_map/ppermute | solution.py:219

commit v2 on v1

v2 whole, which is shorter than its diff:
```python
import jax
import jax.numpy as jnp
from jax import lax
from jax.experimental import pallas as pl
from jax.experimental.pallas import tpu as pltpu
from jax.sharding import Mesh, PartitionSpec as P

SLICES = 4
CORES = 2
LANES = 128
MAIN = 8
VMEM = pltpu.VMEM
F32 = jnp.float32
BF16 = jnp.bfloat16


def whole(count):
    return [pl.BlockSpec(memory_space=VMEM)] * count


def apart(count):
    return [pl.BlockSpec(memory_space=pltpu.HBM)] * count


def pack_kernel(
    capacity, core_ref, routes_hbm, weight_hbm, tokens_hbm, grad_hbm, out_ref,
    routes_ref, weight_ref, rows_ref, grad_ref, sems,
):
    width, count = grad_ref.shape
    pairs = (
        (routes_hbm, routes_ref),
        (weight_hbm, weight_ref),
        (grad_hbm, grad_ref),
        (tokens_hbm, rows_ref.at[pl.ds(width, width)]),
    )
    copies = [pltpu.make_async_copy(a, b, sems.at[i]) for i, (a, b) in enumerate(pairs)]
    for copy in copies:
        copy.start()
    experts = out_ref.shape[0] // SLICES
    chunks = 2 * width // LANES
    extra = capacity - MAIN
    tail_rows = out_ref.shape[1] - chunks * MAIN
    earlier = lax.broadcasted_iota(jnp.int32, (count, count), 0)
    later = lax.broadcasted_iota(jnp.int32, (count, count), 1)
    order = (earlier < later).astype(F32)
    copies[0].wait()
    expert = routes_ref[...]
    onehot = (expert == lax.broadcasted_iota(jnp.int32, (experts, count), 0)).astype(F32)
    before = jnp.dot(onehot, order, preferred_element_type=F32)
    slot = jnp.sum(onehot * before, axis=0, keepdims=True).astype(jnp.int32)
    contract = (((1,), (1,)), ((), ()))
    place = lax.broadcasted_iota(jnp.int32, (experts * MAIN, count), 0)
    main_pick = ((slot < MAIN) & (expert * MAIN + slot == place)).astype(F32).astype(BF16)
    for copy in copies[1:]:
        copy.wait()
    rows_ref[:width] = (weight_ref[...].astype(F32) * grad_ref[...].astype(F32)).astype(BF16)
    main = lax.dot_general(main_pick, rows_ref[...], contract, preferred_element_type=F32)
    place = lax.broadcasted_iota(jnp.int32, (experts * tail_rows, count), 0)
    tail = jnp.zeros((experts * tail_rows, LANES), F32)
    for c in range(chunks):
        target = expert * tail_rows + c * extra + slot - MAIN
        pick = ((slot >= MAIN) & (target == place)).astype(F32).astype(BF16)
        tail = tail + lax.dot_general(
            pick, rows_ref[c * LANES : (c + 1) * LANES], contract, preferred_element_type=F32
        )
    for e in range(experts):
        pieces = [
            main[e * MAIN : (e + 1) * MAIN, c * LANES : (c + 1) * LANES] for c in range(chunks)
        ]
        pieces.append(tail[e * tail_rows : (e + 1) * tail_rows])
        block = jnp.concatenate(pieces, axis=0).astype(BF16)
        for copy in range(SLICES):
            seat = e * SLICES + copy
            turned = (seat + out_ref.shape[0] // 2) % out_ref.shape[0]
            out_ref[jnp.where(core_ref[0] == 0, seat, turned)] = block


def multiply(rows_ref, gate_up_ref, down_ref, start, step, out_ref):
    wide, pair = gate_up_ref.shape
    width = rows_ref.shape[1]
    for i in range(out_ref.shape[0] // step):
        at = pl.multiple_of(start + i * step, 16)
        here = slice(i * step, (i + 1) * step)
        out_ref[here, :pair] = jnp.dot(
            rows_ref[pl.ds(at, step), width - wide :], gate_up_ref[...], preferred_element_type=F32
        ).astype(BF16)
        out_ref[here, pair:] = jnp.dot(
            rows_ref[pl.ds(at, step), :wide], down_ref[...], preferred_element_type=F32
        ).astype(BF16)


def send_kernel(
    capacity, step, core_ref, arrived_ref, gate_hbm, up_hbm, down_hbm,
    rows_ref, send_ref, gate_up_ref, down_ref, sems,
):
    sources, block_rows, _ = arrived_ref.shape
    slots, width = rows_ref.shape
    half = slots // CORES
    chunks = width // LANES
    depth, hidden = gate_hbm.shape
    wide = gate_up_ref.shape[0]
    extra = capacity - MAIN
    tail_rows = block_rows - chunks * MAIN
    pairs = (
        (gate_hbm, gate_up_ref.at[pl.ds(wide - depth, depth), pl.ds(0, hidden)]),
        (up_hbm, gate_up_ref.at[pl.ds(wide - depth, depth), pl.ds(hidden, hidden)]),
        (down_hbm, down_ref.at[pl.ds(0, depth)]),
    )
    copies = [pltpu.make_async_copy(a, b, sems.at[i]) for i, (a, b) in enumerate(pairs)]
    for copy in copies:
        copy.start()
    gate_up_ref[: wide - depth] = jnp.zeros((wide - depth, 2 * hidden), BF16)
    down_ref[depth:] = jnp.zeros((wide - depth, hidden), BF16)

    turn = core_ref[0] * (sources // 2)
    block_of = lambda source: arrived_ref[lax.rem(turn + source, sources)].astype(F32)

    def unpack(pair, carry):
        first = block_of(2 * pair)[: chunks * MAIN]
        second = block_of(2 * pair + 1)[: chunks * MAIN]
        at = pl.multiple_of(pair * 2 * MAIN, 2 * MAIN)
        for c in range(chunks):
            both = jnp.concatenate(
                [first[c * MAIN : (c + 1) * MAIN], second[c * MAIN : (c + 1) * MAIN]], axis=0
            )
            rows_ref[pl.ds(at, 2 * MAIN), c * LANES : (c + 1) * LANES] = both.astype(BF16)
        return carry

    lax.fori_loop(0, sources // 2, unpack, 0, unroll=4)
    group = 16
    place = lax.broadcasted_iota(jnp.int32, (chunks * group * extra, group * tail_rows), 0)
    origin = lax.broadcasted_iota(jnp.int32, (chunks * group * extra, group * tail_rows), 1)
    chunk = place // (group * extra)
    inside = place % (group * extra)
    wanted = (inside // extra) * tail_rows + chunk * extra + inside % extra
    pick = (wanted == origin).astype(F32).astype(BF16)
    for g in range(sources // group):
        tails = [block_of(g * group + s)[chunks * MAIN :] for s in range(group)]
        tail = jnp.concatenate(tails, axis=0).astype(BF16)
        moved = jnp.dot(pick, tail, preferred_element_type=F32).astype(BF16)
        at = sources * MAIN + g * group * extra
        for c in range(chunks):
            rows_ref[at : at + group * extra, c * LANES : (c + 1) * LANES] = moved[
                c * group * extra : (c + 1) * group * extra
            ]
    for copy in copies:
        copy.wait()
    multiply(rows_ref, gate_up_ref, down_ref, (1 - core_ref[0]) * half, step, send_ref)


def keep_kernel(step, core_ref, rows_ref, gate_up_ref, down_ref, keep_ref):
    multiply(rows_ref, gate_up_ref, down_ref, core_ref[0] * keep_ref.shape[0], step, keep_ref)


def factor_kernel(parts_ref, out_ref):
    parts, _, columns = parts_ref.shape
    hidden = columns // 3
    total = parts_ref[0].astype(F32)
    for j in range(1, parts):
        total = total + parts_ref[j].astype(F32)
    gate_pre = total[:, :hidden]
    up_pre = total[:, hidden : 2 * hidden]
    act_grad = total[:, 2 * hidden :]
    sigmoid = 1.0 / (1.0 + jnp.exp(-gate_pre))
    gate_grad = (act_grad * up_pre * sigmoid * (1.0 + gate_pre * (1.0 - sigmoid))).astype(BF16)
    up_grad = (act_grad * gate_pre * sigmoid).astype(BF16)
    for j in range(out_ref.shape[0]):
        out_ref[j, :, :hidden] = gate_grad
        out_ref[j, :, hidden:] = up_grad


def outer(rows_ref, factor_ref, start, wide):
    half = factor_ref.shape[0]
    rows = rows_ref[pl.ds(pl.multiple_of(start, 16), half), rows_ref.shape[1] - wide :]
    return lax.dot_general(
        rows, factor_ref[...], (((0,), (0,)), ((), ())), preferred_element_type=F32
    )


def own_kernel(core_ref, rows_ref, own_ref, total_ref):
    start = core_ref[0] * own_ref.shape[0]
    total_ref[...] = outer(rows_ref, own_ref, start, total_ref.shape[0])


def other_kernel(core_ref, rows_ref, other_ref, total_ref, gate_ref, up_ref):
    wide = total_ref.shape[0]
    depth, hidden = gate_ref.shape
    start = (1 - core_ref[0]) * other_ref.shape[0]
    total = total_ref[...] + outer(rows_ref, other_ref, start, wide)
    gate_ref[...] = total[wide - depth :, :hidden].astype(BF16)
    up_ref[...] = total[wide - depth :, hidden:].astype(BF16)


def shards(tokens, routes, route_weight, out_grad, w_gate, w_up, w_down):
    columns = lax.axis_size("expert")
    chips = lax.axis_size("chip")
    experts = columns // SLICES
    count, depth = tokens.shape
    hidden = w_gate.shape[1]
    width = 2 * depth
    chunks = width // LANES
    capacity = max(2, count * 5 // (experts * 4))
    slots = columns * capacity
    half = slots // CORES
    block_rows = chunks * MAIN + -(-chunks * (capacity - MAIN) // 8) * 8
    wide = -(-depth // LANES) * LANES
    core = lax.axis_index("core").astype(jnp.int32).reshape(1)
    turned = [*range(columns // 2, columns), *range(columns // 2)]
    planes = [[e * CORES for e in range(columns)], [e * CORES + 1 for e in turned]]
    walk = [*range(0, chips, 2), *range(1, chips, 2)]
    rings = [[chip * CORES for chip in walk], [chip * CORES + 1 for chip in reversed(walk)]]
    pairs = [(c, (c + 1) % CORES) for c in range(CORES)]
    smem = pl.BlockSpec(memory_space=pltpu.SMEM)

    limit = pltpu.CompilerParams(vmem_limit_bytes=24 << 20)
    most = pltpu.CompilerParams(vmem_limit_bytes=56 << 20)

    blocks = pl.pallas_call(
        lambda *refs: pack_kernel(capacity, *refs),
        out_shape=jax.ShapeDtypeStruct((columns, block_rows, LANES), BF16),
        in_specs=[smem] + apart(4),
        out_specs=whole(1)[0],
        scratch_shapes=[
            VMEM((1, count), jnp.int32),
            VMEM((1, count), BF16),
            VMEM((width, count), BF16),
            VMEM((depth, count), BF16),
            pltpu.SemaphoreType.DMA((4,)),
        ],
        compiler_params=most,
        name="pack",
    )(core, routes.T, route_weight.T, tokens.T, out_grad.T)
    arrived = lax.all_to_all(
        blocks, ("expert", "core"), split_axis=0, concat_axis=0, axis_index_groups=planes, tiled=True
    )
    rows, send, gate_up, down = pl.pallas_call(
        lambda *refs: send_kernel(capacity, 80, *refs),
        out_shape=(
            jax.ShapeDtypeStruct((slots, width), BF16),
            jax.ShapeDtypeStruct((half, 3 * hidden), BF16),
            jax.ShapeDtypeStruct((wide, 2 * hidden), BF16),
            jax.ShapeDtypeStruct((wide, hidden), BF16),
        ),
        in_specs=[smem] + whole(1) + apart(3),
        out_specs=tuple(whole(4)),
        scratch_shapes=[pltpu.SemaphoreType.DMA((3,))],
        compiler_params=limit,
        name="send",
    )(core, arrived, w_gate, w_up, w_down.T)
    sibling = lax.ppermute(send, "core", pairs)
    keep = pl.pallas_call(
        lambda *refs: keep_kernel(80, *refs),
        out_shape=jax.ShapeDtypeStruct((half, 3 * hidden), BF16),
        in_specs=[smem] + whole(3),
        out_specs=whole(1)[0],
        compiler_params=limit,
        cost_estimate=pl.CostEstimate(
            flops=6 * half * wide * hidden, bytes_accessed=8 << 20, transcendentals=0
        ),
        name="keep",
    )(core, rows, gate_up, down)
    summed = (keep.astype(F32) + sibling.astype(F32)).astype(BF16)
    parts = lax.all_to_all(
        summed.reshape(chips, half // chips, 3 * hidden),
        ("chip", "core"), split_axis=0, concat_axis=0, axis_index_groups=rings, tiled=True,
    )
    spread = pl.pallas_call(
        factor_kernel,
        out_shape=jax.ShapeDtypeStruct((chips, half // chips, 2 * hidden), BF16),
        in_specs=whole(1),
        out_specs=whole(1)[0],
        compiler_params=limit,
        name="factor",
    )(parts)
    own = lax.all_to_all(
        spread, ("chip", "core"), split_axis=0, concat_axis=0, axis_index_groups=rings, tiled=True
    ).reshape(half, 2 * hidden)
    other = lax.ppermute(own, "core", pairs)
    total = pl.pallas_call(
        own_kernel,
        out_shape=jax.ShapeDtypeStruct((wide, 2 * hidden), F32),
        in_specs=[smem] + whole(2),
        out_specs=whole(1)[0],
        compiler_params=limit,
        cost_estimate=pl.CostEstimate(
            flops=4 * half * wide * hidden, bytes_accessed=8 << 20, transcendentals=0
        ),
        name="own",
    )(core, rows, own)
    return pl.pallas_call(
        other_kernel,
        out_shape=(
            jax.ShapeDtypeStruct((depth, hidden), BF16),
            jax.ShapeDtypeStruct((depth, hidden), BF16),
        ),
        in_specs=[smem] + whole(3),
        out_specs=tuple(whole(2)),
        compiler_params=limit,
        name="other",
    )(core, rows, other, total)


def solution(mesh):
    devices = mesh.devices
    columns, members = devices.shape
    split = Mesh(devices.reshape(columns, members // CORES, CORES), ("expert", "chip", "core"))
    width = ("chip", "core")
    in_specs = (
        P("expert", width),
        P("expert", None),
        P("expert", None),
        P("expert", width),
        P(width, "expert"),
        P(width, "expert"),
        P("expert", width),
    )
    out_specs = (P(width, "expert"), P(width, "expert"))
    return jax.shard_map(shards, mesh=split, in_specs=in_specs, out_specs=out_specs, check_vma=False)
```

time: 133 us -> 126 us (0.947)
  blocking collectives: 53.9 us -> 106 us
  waiting for transfers between devices: 33.8 us -> 1.9 us
  starting transfers between devices: 34.1 us -> 8.2 us
  local copies, waits for them, and re-layouts: 3.11 us -> 0.01 us
  Pallas kernels: 6.63 us -> 8.5 us
    all_to_all x2 -> x3, blocking collectives: 53.9 us -> 106 us  [the longest x1 55.1 us: shards(): lax.all_to_all(blocks, ('expert', 'core'), split_axis=0, concat_axis=0, a...]
    all_to_all x1 -> x0, waiting for transfers between devices: 29.9 us -> none  [shards(): lax.all_to_all(blocks, 'expert', split_axis=0, concat_axis=0, tiled=True)]
    all_to_all x1 -> x0, starting transfers between devices: 23.3 us -> none  [shards(): lax.all_to_all(blocks, 'expert', split_axis=0, concat_axis=0, tiled=True)]
    unnamed x14 -> x6, local copies, waits for them, and re-layouts: 3.11 us -> 0.01 us
    ppermute x1, starting transfers between devices: 5.58 us -> 3.29 us  [shards(): sibling = lax.ppermute(send, 'core', pairs)]
    pallas_call x2 -> x4, Pallas kernels: 4.95 us -> 5.75 us  [the longest x1 2.27 us: shards(): pl.pallas_call(lambda *refs: send_kernel(capacity, 80, *refs), out_shape=...]
  transfers between devices with their start and end apart: 3 -> 2, of which waited for: 3 -> 2; matrix products, arithmetic and copies ran while one was open for 0% -> 0% of each run, Pallas kernels for 0% -> 2%
where the time goes in v2:
time: 126 us
  blocking collectives  106 us (84%)
  Pallas kernels  8.5 us (7%)
  starting transfers between devices  8.2 us (7%)
  waiting for transfers between devices  1.9 us (2%)
    all_to_all x1, blocking collectives, shards(): lax.all_to_all(blocks, ('expert', 'core'), split_axis=0, concat_axis=0, a...  55.1 us
    all_to_all x1, blocking collectives, shards(): lax.all_to_all(summed.reshape(chips, half // chips, 3 * hidden), ('chip',...  30.1 us
    all_to_all x1, blocking collectives, shards(): lax.all_to_all(spread, ('chip', 'core'), split_axis=0, concat_axis=0, axi...  20.9 us
    ppermute x1, starting transfers between devices, shards(): other = lax.ppermute(own, 'core', pairs)  4.91 us
    ppermute x1, starting transfers between devices, shards(): sibling = lax.ppermute(send, 'core', pairs)  3.29 us
    pallas_call x1, Pallas kernels, shards(): pl.pallas_call(lambda *refs: pack_kernel(capacity, *refs), out_shape=jax....  2.58 us
  transfers between devices with their start and end apart: 2, of which 2 were waited for; matrix products, arithmetic and copies ran while one was open for 0% of the time, Pallas kernels for 2%

profile of v2, /device:TPU:1, one launch (start us, length us, event | category | flops | bytes accessed | tf_op | source)
XLA Modules:
  0.0 125.7 jit_solution(5521556636759542121)
XLA Ops:
  0.6 0.0 copy-start.2
  0.6 0.0 copy-start.1
  0.7 0.0 copy-start
  0.7 2.6 %pack.1 = bf16[64,72,128]{2,1,0:T(8,128)(2,1)} custom-call(s32[1]{0:T(128)} %bitcast.refs_0_.core_ref, s32[1,128]{1,0:T(1,128)} %bitcast.14, bf16[1,128]{1,0:T(2,128)(2,1)} %bitcast.15, bf16[448,128]{1,0:T(8,128)(2,1)} %bitcast.12, bf16[448,128]{1,0:T(8,128)(2,1)} %bitcast.13), custom_call_target="tpu_custom_call" | custom-call | tf_op jit(solution)/shard_map/pack/pallas_call | solution.py:218
  3.3 55.1 %all_to_all.15.refs_1_ = bf16[64,72,128]{2,1,0:T(8,128)(2,1)S(1)} all-to-all(bf16[64,72,128]{2,1,0:T(8,128)(2,1)} %pack.1), channel_id=1, replica_groups={{0,16,32,48,64,80,96,112,128,144,160,176,192,208,224,240,256,272,288,30..., dimensions={0} | all-to-all | bytes 2359296 | tf_op jit(solution)/shard_map/all_to_all | solution.py:233
  58.4 0.0 copy-done.2
  58.4 0.0 copy-done.1
  58.4 0.0 copy-done
  58.4 2.3 %send.1 = (bf16[640,896]{1,0:T(8,128)(2,1)S(1)}, bf16[320,1536]{1,0:T(8,128)(2,1)S(1)}, bf16[512,1024]{1,0:T(8,128)(2,1)S(1)}, bf16[512,512]{1,0:T(8,128)(2,1)S(1)}) custom-call(s32[1]{0:T(128)} %bitcast.refs_0_.core_ref, bf16[64,72,128]{2,1,0:T(8,128)(2,1)S(1)} %all_to_all.15.refs_1_, bf16[448,512]{1,0:T(8,128)(2,1)S(1)} %copy-done, ...), custom_call_target="tpu_custom_call" | custom-call | tf_op jit(solution)/shard_map/send/pallas_call | solution.py:236
  60.7 3.3 %collective-permute-start = (bf16[320,1536]{1,0:T(8,128)(2,1)S(1)}, bf16[320,1536]{1,0:T(8,128)(2,1)S(1)}, u32[]{:S(2)}, u32[]{:S(2)}) collective-permute-start(bf16[320,1536]{1,0:T(8,128)(2,1)S(1)} %get-tuple-element.9), channel_id=1, source_target_pairs={{0,1},{1,0},{2,3},{3,2},{4,5},{5,4},{6,7},{7,6},{8,9},{9,8},{10,11... | collective-permute-start | bytes 2949128 | tf_op jit(solution)/shard_map/ppermute | solution.py:250
  64.0 1.2 keep.1
  65.2 0.9 collective-permute-done
  66.1 0.2 add_convert_fusion
  66.4 30.1 %all_to_all.16.parts_ref = bf16[8,40,1536]{2,1,0:T(8,128)(2,1)S(1)} all-to-all(bf16[8,40,1536]{2,1,0:T(8,128)(2,1)S(1)} %bitcast.11), channel_id=1, replica_groups={{0,4,8,12,2,6,10,14},{15,11,7,3,13,9,5,1},{16,20,24,28,18,22,26,30},{31..., dimensions={0} | all-to-all | bytes 1966080 | tf_op jit(solution)/shard_map/all_to_all | solution.py:263
  96.5 0.2 factor.1
  96.6 20.9 %all_to_all.17 = bf16[8,40,1024]{2,1,0:T(8,128)(2,1)S(1)} all-to-all(bf16[8,40,1024]{2,1,0:T(8,128)(2,1)S(1)} %factor.1), channel_id=1, replica_groups={{0,4,8,12,2,6,10,14},{15,11,7,3,13,9,5,1},{16,20,24,28,18,22,26,30},{31..., dimensions={0} | all-to-all | bytes 1310720 | tf_op jit(solution)/shard_map/all_to_all | solution.py:275
  117.5 4.9 %collective-permute-start.1 = (bf16[320,1024]{1,0:T(8,128)(2,1)S(1)}, bf16[320,1024]{1,0:T(8,128)(2,1)S(1)}, u32[]{:S(2)}, u32[]{:S(2)}) collective-permute-start(bf16[320,1024]{1,0:T(8,128)(2,1)S(1)} %bitcast.8), channel_id=1, source_target_pairs={{0,1},{1,0},{2,3},{3,2},{4,5},{5,4},{6,7},{7,6},{8,9},{9,8},{10,11... | collective-permute-start | bytes 1966088 | tf_op jit(solution)/shard_map/ppermute | solution.py:278
  122.4 0.7 own.1.total_ref
  123.2 1.0 collective-permute-done.1.other_ref
  124.1 1.5 %other.1 = (bf16[448,512]{1,0:T(8,128)(2,1)}, bf16[448,512]{1,0:T(8,128)(2,1)}) custom-call(s32[1]{0:T(128)} %bitcast.refs_0_.core_ref, bf16[640,896]{1,0:T(8,128)(2,1)S(1)} %get-tuple-element.6.refs_1_.rows_ref, bf16[320,1024]{1,0:T(8,128)(2,1)S(1)} %collective-permute-done.1.other_ref, f32[512,1024]{1,0:T(8,128)S(1)} %own.1.total_ref), custom_call_target="tpu_custom_call" | custom-call | tf_op jit(solution)/shard_map/other/pallas_call | solution.py:290
Async XLA Ops:
  0.6 57.7 %copy-start.2 = (bf16[512,448]{0,1:T(8,128)(2,1)S(1)}, bf16[512,448]{0,1:T(8,128)(2,1)}, u32[]{:S(2)}) copy-start(bf16[512,448]{0,1:T(8,128)(2,1)} %param.13) | copy-start | bytes 1376260
  0.6 57.7 %copy-start.1 = (bf16[448,512]{1,0:T(8,128)(2,1)S(1)}, bf16[448,512]{1,0:T(8,128)(2,1)}, u32[]{:S(2)}) copy-start(bf16[448,512]{1,0:T(8,128)(2,1)} %refs_3_.1) | copy-start | bytes 1376260
  0.7 57.7 %copy-start = (bf16[448,512]{1,0:T(8,128)(2,1)S(1)}, bf16[448,512]{1,0:T(8,128)(2,1)}, u32[]{:S(2)}) copy-start(bf16[448,512]{1,0:T(8,128)(2,1)} %refs_2_.1) | copy-start | bytes 1376260
  60.7 5.5 %collective-permute-start = (bf16[320,1536]{1,0:T(8,128)(2,1)S(1)}, bf16[320,1536]{1,0:T(8,128)(2,1)S(1)}, u32[]{:S(2)}, u32[]{:S(2)}) collective-permute-start(bf16[320,1536]{1,0:T(8,128)(2,1)S(1)} %get-tuple-element.9), channel_id=1, source_target_pairs={{0,1},{1,0},{2,3},{3,2},{4,5},{5,4},{6,7},{7,6},{8,9},{9,8},{10,11... | collective-permute-start | bytes 2949128 | tf_op jit(solution)/shard_map/ppermute | solution.py:250
  117.5 6.6 %collective-permute-start.1 = (bf16[320,1024]{1,0:T(8,128)(2,1)S(1)}, bf16[320,1024]{1,0:T(8,128)(2,1)S(1)}, u32[]{:S(2)}, u32[]{:S(2)}) collective-permute-start(bf16[320,1024]{1,0:T(8,128)(2,1)S(1)} %bitcast.8), channel_id=1, source_target_pairs={{0,1},{1,0},{2,3},{3,2},{4,5},{5,4},{6,7},{7,6},{8,9},{9,8},{10,11... | collective-permute-start | bytes 1966088 | tf_op jit(solution)/shard_map/ppermute | solution.py:278

commit v3 on v2

--- a/solution.py
+++ b/solution.py
@@ -71,21 +71,60 @@
         block = jnp.concatenate(pieces, axis=0).astype(BF16)
         for copy in range(SLICES):
             seat = e * SLICES + copy
-            turned = (seat + out_ref.shape[0] // 2) % out_ref.shape[0]
-            out_ref[jnp.where(core_ref[0] == 0, seat, turned)] = block
-
-
-def multiply(rows_ref, gate_up_ref, down_ref, start, step, out_ref):
+            last = out_ref.shape[0] - 1 - seat
+            out_ref[jnp.where(core_ref[0] == 0, seat, last)] = block
+
+
+def unpack(capacity, core_ref, half, arrived_ref, rows_ref):
+    sources, block_rows, _ = arrived_ref.shape
+    width = rows_ref.shape[1]
+    members = sources // CORES
+    chunks = width // LANES
+    extra = capacity - MAIN
+    tail_rows = block_rows - chunks * MAIN
+    first_core = core_ref[0] == 0
+
+    def block_of(source):
+        source = half * members + source
+        return arrived_ref[jnp.where(first_core, source, sources - 1 - source)].astype(F32)
+
+    def main_rows(pair, carry):
+        first = block_of(2 * pair)
+        second = block_of(2 * pair + 1)
+        at = pl.multiple_of(pair * 2 * MAIN, 2 * MAIN)
+        for c in range(chunks):
+            here = slice(c * MAIN, (c + 1) * MAIN)
+            both = jnp.concatenate([first[here], second[here]], axis=0)
+            rows_ref[pl.ds(at, 2 * MAIN), c * LANES : (c + 1) * LANES] = both.astype(BF16)
+        return carry
+
+    lax.fori_loop(0, members // 2, main_rows, 0, unroll=4)
+    group = 16
+    size = group * extra
+    place = lax.broadcasted_iota(jnp.int32, (chunks * size, group * tail_rows), 0)
+    origin = lax.broadcasted_iota(jnp.int32, (chunks * size, group * tail_rows), 1)
+    inside = place % size
+    wanted = (inside // extra) * tail_rows + place // size * extra + inside % extra
+    pick = (wanted == origin).astype(F32).astype(BF16)
+    for g in range(members // group):
+        tails = [block_of(g * group + s)[chunks * MAIN :] for s in range(group)]
+        tail = jnp.concatenate(tails, axis=0).astype(BF16)
+        moved = jnp.dot(pick, tail, preferred_element_type=F32).astype(BF16)
+        at = members * MAIN + g * size
+        for c in range(chunks):
+            rows_ref[at : at + size, c * LANES : (c + 1) * LANES] = moved[c * size : (c + 1) * size]
+
+
+def multiply(rows_ref, gate_up_ref, down_ref, step, out_ref):
     wide, pair = gate_up_ref.shape
     width = rows_ref.shape[1]
-    for i in range(out_ref.shape[0] // step):
-        at = pl.multiple_of(start + i * step, 16)
-        here = slice(i * step, (i + 1) * step)
+    for at in range(0, out_ref.shape[0], step):
+        here = slice(at, at + step)
         out_ref[here, :pair] = jnp.dot(
-            rows_ref[pl.ds(at, step), width - wide :], gate_up_ref[...], preferred_element_type=F32
+            rows_ref[here, width - wide :], gate_up_ref[...], preferred_element_type=F32
         ).astype(BF16)
         out_ref[here, pair:] = jnp.dot(
-            rows_ref[pl.ds(at, step), :wide], down_ref[...], preferred_element_type=F32
+            rows_ref[here, :wide], down_ref[...], preferred_element_type=F32
         ).astype(BF16)
 
 
@@ -93,14 +132,8 @@
     capacity, step, core_ref, arrived_ref, gate_hbm, up_hbm, down_hbm,
     rows_ref, send_ref, gate_up_ref, down_ref, sems,
 ):
-    sources, block_rows, _ = arrived_ref.shape
-    slots, width = rows_ref.shape
-    half = slots // CORES
-    chunks = width // LANES
     depth, hidden = gate_hbm.shape
     wide = gate_up_ref.shape[0]
-    extra = capacity - MAIN
-    tail_rows = block_rows - chunks * MAIN
     pairs = (
         (gate_hbm, gate_up_ref.at[pl.ds(wide - depth, depth), pl.ds(0, hidden)]),
         (up_hbm, gate_up_ref.at[pl.ds(wide - depth, depth), pl.ds(hidden, hidden)]),
@@ -111,45 +144,15 @@
         copy.start()
     gate_up_ref[: wide - depth] = jnp.zeros((wide - depth, 2 * hidden), BF16)
     down_ref[depth:] = jnp.zeros((wide - depth, hidden), BF16)
-
-    turn = core_ref[0] * (sources // 2)
-    block_of = lambda source: arrived_ref[lax.rem(turn + source, sources)].astype(F32)
-
-    def unpack(pair, carry):
-        first = block_of(2 * pair)[: chunks * MAIN]
-        second = block_of(2 * pair + 1)[: chunks * MAIN]
-        at = pl.multiple_of(pair * 2 * MAIN, 2 * MAIN)
-        for c in range(chunks):
-            both = jnp.concatenate(
-                [first[c * MAIN : (c + 1) * MAIN], second[c * MAIN : (c + 1) * MAIN]], axis=0
-            )
-            rows_ref[pl.ds(at, 2 * MAIN), c * LANES : (c + 1) * LANES] = both.astype(BF16)
-        return carry
-
-    lax.fori_loop(0, sources // 2, unpack, 0, unroll=4)
-    group = 16
-    place = lax.broadcasted_iota(jnp.int32, (chunks * group * extra, group * tail_rows), 0)
-    origin = lax.broadcasted_iota(jnp.int32, (chunks * group * extra, group * tail_rows), 1)
-    chunk = place // (group * extra)
-    inside = place % (group * extra)
-    wanted = (inside // extra) * tail_rows + chunk * extra + inside % extra
-    pick = (wanted == origin).astype(F32).astype(BF16)
-    for g in range(sources // group):
-        tails = [block_of(g * group + s)[chunks * MAIN :] for s in range(group)]
-        tail = jnp.concatenate(tails, axis=0).astype(BF16)
-        moved = jnp.dot(pick, tail, preferred_element_type=F32).astype(BF16)
-        at = sources * MAIN + g * group * extra
-        for c in range(chunks):
-            rows_ref[at : at + group * extra, c * LANES : (c + 1) * LANES] = moved[
-                c * group * extra : (c + 1) * group * extra
-            ]
+    unpack(capacity, core_ref, 1 - core_ref[0], arrived_ref, rows_ref)
     for copy in copies:
         copy.wait()
-    multiply(rows_ref, gate_up_ref, down_ref, (1 - core_ref[0]) * half, step, send_ref)
-
-
-def keep_kernel(step, core_ref, rows_ref, gate_up_ref, down_ref, keep_ref):
-    multiply(rows_ref, gate_up_ref, down_ref, core_ref[0] * keep_ref.shape[0], step, keep_ref)
+    multiply(rows_ref, gate_up_ref, down_ref, step, send_ref)
+
+
+def keep_kernel(capacity, step, core_ref, arrived_ref, gate_up_ref, down_ref, rows_ref, keep_ref):
+    unpack(capacity, core_ref, core_ref[0], arrived_ref, rows_ref)
+    multiply(rows_ref, gate_up_ref, down_ref, step, keep_ref)
 
 
 def factor_kernel(parts_ref, out_ref):
@@ -169,24 +172,21 @@
         out_ref[j, :, hidden:] = up_grad
 
 
-def outer(rows_ref, factor_ref, start, wide):
-    half = factor_ref.shape[0]
-    rows = rows_ref[pl.ds(pl.multiple_of(start, 16), half), rows_ref.shape[1] - wide :]
+def outer(rows_ref, factor_ref, wide):
+    rows = rows_ref[:, rows_ref.shape[1] - wide :]
     return lax.dot_general(
         rows, factor_ref[...], (((0,), (0,)), ((), ())), preferred_element_type=F32
     )
 
 
-def own_kernel(core_ref, rows_ref, own_ref, total_ref):
-    start = core_ref[0] * own_ref.shape[0]
-    total_ref[...] = outer(rows_ref, own_ref, start, total_ref.shape[0])
-
-
-def other_kernel(core_ref, rows_ref, other_ref, total_ref, gate_ref, up_ref):
+def own_kernel(rows_ref, own_ref, total_ref):
+    total_ref[...] = outer(rows_ref, own_ref, total_ref.shape[0])
+
+
+def other_kernel(rows_ref, other_ref, total_ref, gate_ref, up_ref):
     wide = total_ref.shape[0]
     depth, hidden = gate_ref.shape
-    start = (1 - core_ref[0]) * other_ref.shape[0]
-    total = total_ref[...] + outer(rows_ref, other_ref, start, wide)
+    total = total_ref[...] + outer(rows_ref, other_ref, wide)
     gate_ref[...] = total[wide - depth :, :hidden].astype(BF16)
     up_ref[...] = total[wide - depth :, hidden:].astype(BF16)
 
@@ -205,9 +205,9 @@
     block_rows = chunks * MAIN + -(-chunks * (capacity - MAIN) // 8) * 8
     wide = -(-depth // LANES) * LANES
     core = lax.axis_index("core").astype(jnp.int32).reshape(1)
-    turned = [*range(columns // 2, columns), *range(columns // 2)]
-    planes = [[e * CORES for e in range(columns)], [e * CORES + 1 for e in turned]]
-    walk = [*range(0, chips, 2), *range(1, chips, 2)]
+    line = list(range(columns))
+    planes = [[e * CORES for e in line], [e * CORES + 1 for e in reversed(line)]]
+    walk = list(range(chips))
     rings = [[chip * CORES for chip in walk], [chip * CORES + 1 for chip in reversed(walk)]]
     pairs = [(c, (c + 1) % CORES) for c in range(CORES)]
     smem = pl.BlockSpec(memory_space=pltpu.SMEM)
@@ -233,10 +233,10 @@
     arrived = lax.all_to_all(
         blocks, ("expert", "core"), split_axis=0, concat_axis=0, axis_index_groups=planes, tiled=True
     )
-    rows, send, gate_up, down = pl.pallas_call(
-        lambda *refs: send_kernel(capacity, 80, *refs),
+    other_rows, send, gate_up, down = pl.pallas_call(
+        lambda *refs: send_kernel(capacity, 320, *refs),
         out_shape=(
-            jax.ShapeDtypeStruct((slots, width), BF16),
+            jax.ShapeDtypeStruct((half, width), BF16),
             jax.ShapeDtypeStruct((half, 3 * hidden), BF16),
             jax.ShapeDtypeStruct((wide, 2 * hidden), BF16),
             jax.ShapeDtypeStruct((wide, hidden), BF16),
@@ -248,17 +248,20 @@
         name="send",
     )(core, arrived, w_gate, w_up, w_down.T)
     sibling = lax.ppermute(send, "core", pairs)
-    keep = pl.pallas_call(
-        lambda *refs: keep_kernel(80, *refs),
-        out_shape=jax.ShapeDtypeStruct((half, 3 * hidden), BF16),
+    own_rows, keep = pl.pallas_call(
+        lambda *refs: keep_kernel(capacity, 320, *refs),
+        out_shape=(
+            jax.ShapeDtypeStruct((half, width), BF16),
+            jax.ShapeDtypeStruct((half, 3 * hidden), BF16),
+        ),
         in_specs=[smem] + whole(3),
-        out_specs=whole(1)[0],
+        out_specs=tuple(whole(2)),
         compiler_params=limit,
         cost_estimate=pl.CostEstimate(
             flops=6 * half * wide * hidden, bytes_accessed=8 << 20, transcendentals=0
         ),
         name="keep",
-    )(core, rows, gate_up, down)
+    )(core, arrived, gate_up, down)
     summed = (keep.astype(F32) + sibling.astype(F32)).astype(BF16)
     parts = lax.all_to_all(
         summed.reshape(chips, half // chips, 3 * hidden),
@@ -279,25 +282,25 @@
     total = pl.pallas_call(
         own_kernel,
         out_shape=jax.ShapeDtypeStruct((wide, 2 * hidden), F32),
-        in_specs=[smem] + whole(2),
+        in_specs=whole(2),
         out_specs=whole(1)[0],
         compiler_params=limit,
         cost_estimate=pl.CostEstimate(
             flops=4 * half * wide * hidden, bytes_accessed=8 << 20, transcendentals=0
         ),
         name="own",
-    )(core, rows, own)
+    )(own_rows, own)
     return pl.pallas_call(
         other_kernel,
         out_shape=(
             jax.ShapeDtypeStruct((depth, hidden), BF16),
             jax.ShapeDtypeStruct((depth, hidden), BF16),
         ),
-        in_specs=[smem] + whole(3),
+        in_specs=whole(3),
         out_specs=tuple(whole(2)),
         compiler_params=limit,
         name="other",
-    )(core, rows, other, total)
+    )(other_rows, other, total)
 
 
 def solution(mesh):

time: 126 us -> 123 us (0.976)
  blocking collectives: 106 us -> 102 us
    all_to_all x1, blocking collectives: 55.1 us -> 52 us  [shards(): lax.all_to_all(blocks, ('expert', 'core'), split_axis=0, concat_axis=0, a...]
    all_to_all x1, blocking collectives: 30.1 us -> 28.3 us  [shards(): lax.all_to_all(summed.reshape(chips, half // chips, 3 * hidden), ('chip',...]
  transfers between devices with their start and end apart: 2 -> 2, of which waited for: 2 -> 2; matrix products, arithmetic and copies ran while one was open for 0% -> 0% of each run, Pallas kernels for 2% -> 1%
where the time goes in v3:
time: 123 us; the launch traced here: 121 us
  blocking collectives  102 us (83%)
  starting transfers between devices  8.98 us (7%)
  Pallas kernels  7.35 us (6%)
  waiting for transfers between devices  2.2 us (2%)
    all_to_all x1, blocking collectives, shards(): lax.all_to_all(blocks, ('expert', 'core'), split_axis=0, concat_axis=0, a...  52 us
    all_to_all x1, blocking collectives, shards(): lax.all_to_all(summed.reshape(chips, half // chips, 3 * hidden), ('chip',...  28.3 us
    all_to_all x1, blocking collectives, shards(): lax.all_to_all(spread, ('chip', 'core'), split_axis=0, concat_axis=0, axi...  21.6 us
    ppermute x1, starting transfers between devices, shards(): other = lax.ppermute(own, 'core', pairs)  5.85 us
    ppermute x1, starting transfers between devices, shards(): sibling = lax.ppermute(send, 'core', pairs)  3.13 us
    pallas_call x1, Pallas kernels, shards(): pl.pallas_call(lambda *refs: pack_kernel(capacity, *refs), out_shape=jax....  2.59 us
  transfers between devices with their start and end apart: 2, of which 2 were waited for; matrix products, arithmetic and copies ran while one was open for 0% of the time, Pallas kernels for 1%

profile of v3, /device:TPU:1, one launch (start us, length us, event | category | flops | bytes accessed | tf_op | source)
XLA Modules:
  0.0 121.4 jit_solution(6009889015730489306)
XLA Ops:
  0.6 0.0 copy-start.2
  0.6 0.0 copy-start.1
  0.7 0.0 copy-start
  0.7 2.6 %pack.1 = bf16[64,72,128]{2,1,0:T(8,128)(2,1)} custom-call(s32[1]{0:T(128)} %bitcast.refs_0_, s32[1,128]{1,0:T(1,128)} %bitcast.14, bf16[1,128]{1,0:T(2,128)(2,1)} %bitcast.15, bf16[448,128]{1,0:T(8,128)(2,1)} %bitcast.12, bf16[448,128]{1,0:T(8,128)(2,1)} %bitcast.13), custom_call_target="tpu_custom_call" | custom-call | tf_op jit(solution)/shard_map/pack/pallas_call | solution.py:218
  3.3 52.0 %all_to_all.15.refs_1_ = bf16[64,72,128]{2,1,0:T(8,128)(2,1)S(1)} all-to-all(bf16[64,72,128]{2,1,0:T(8,128)(2,1)} %pack.1), channel_id=1, replica_groups={{0,16,32,48,64,80,96,112,128,144,160,176,192,208,224,240,256,272,288,30..., dimensions={0} | all-to-all | bytes 2359296 | tf_op jit(solution)/shard_map/all_to_all | solution.py:233
  55.2 0.0 copy-done.2
  55.2 0.0 copy-done.1
  55.2 0.0 copy-done
  55.2 1.4 %send.1 = (bf16[320,896]{1,0:T(8,128)(2,1)S(1)}, bf16[320,1536]{1,0:T(8,128)(2,1)S(1)}, bf16[512,1024]{1,0:T(8,128)(2,1)S(1)}, bf16[512,512]{1,0:T(8,128)(2,1)S(1)}) custom-call(s32[1]{0:T(128)} %bitcast.refs_0_, bf16[64,72,128]{2,1,0:T(8,128)(2,1)S(1)} %all_to_all.15.refs_1_, bf16[448,512]{1,0:T(8,128)(2,1)S(1)} %copy-done, bf16[448,512]{1,0:T(8,128)(2,1)S(1)} %copy-done.1, ...), custom_call_target="tpu_custom_call" | custom-call | tf_op jit(solution)/shard_map/send/pallas_call | solution.py:236
  56.7 3.1 %collective-permute-start = (bf16[320,1536]{1,0:T(8,128)(2,1)S(1)}, bf16[320,1536]{1,0:T(8,128)(2,1)S(1)}, u32[]{:S(2)}, u32[]{:S(2)}) collective-permute-start(bf16[320,1536]{1,0:T(8,128)(2,1)S(1)} %get-tuple-element.12), channel_id=1, source_target_pairs={{0,1},{1,0},{2,3},{3,2},{4,5},{5,4},{6,7},{7,6},{8,9},{9,8},{10,11... | collective-permute-start | bytes 2949128 | tf_op jit(solution)/shard_map/ppermute | solution.py:250
  59.8 0.9 keep.1
  60.7 1.2 %collective-permute-done = bf16[320,1536]{1,0:T(8,128)(2,1)S(1)} collective-permute-done((bf16[320,1536]{1,0:T(8,128)(2,1)S(1)}, bf16[320,1536]{1,0:T(8,128)(2,1)S(1)}, u32[]{:S(2)}, u32[]{:S(2)}) %collective-permute-start) | collective-permute-done | bytes 983072 | tf_op jit(solution)/shard_map/ppermute | solution.py:250
  62.0 0.2 add_convert_fusion
  62.2 28.3 %all_to_all.16.parts_ref = bf16[8,40,1536]{2,1,0:T(8,128)(2,1)S(1)} all-to-all(bf16[8,40,1536]{2,1,0:T(8,128)(2,1)S(1)} %bitcast.11), channel_id=1, replica_groups={{0,2,4,6,8,10,12,14},{15,13,11,9,7,5,3,1},{16,18,20,22,24,26,28,30},{31..., dimensions={0} | all-to-all | bytes 1966080 | tf_op jit(solution)/shard_map/all_to_all | solution.py:266
  90.5 0.2 factor.1
  90.7 21.6 %all_to_all.17 = bf16[8,40,1024]{2,1,0:T(8,128)(2,1)S(1)} all-to-all(bf16[8,40,1024]{2,1,0:T(8,128)(2,1)S(1)} %factor.1), channel_id=1, replica_groups={{0,2,4,6,8,10,12,14},{15,13,11,9,7,5,3,1},{16,18,20,22,24,26,28,30},{31..., dimensions={0} | all-to-all | bytes 1310720 | tf_op jit(solution)/shard_map/all_to_all | solution.py:278
  112.3 5.9 %collective-permute-start.1 = (bf16[320,1024]{1,0:T(8,128)(2,1)S(1)}, bf16[320,1024]{1,0:T(8,128)(2,1)S(1)}, u32[]{:S(2)}, u32[]{:S(2)}) collective-permute-start(bf16[320,1024]{1,0:T(8,128)(2,1)S(1)} %bitcast.8), channel_id=1, source_target_pairs={{0,1},{1,0},{2,3},{3,2},{4,5},{5,4},{6,7},{7,6},{8,9},{9,8},{10,11... | collective-permute-start | bytes 1966088 | tf_op jit(solution)/shard_map/ppermute | solution.py:281
  118.2 0.7 own.1.total_ref
  118.9 1.0 collective-permute-done.1.other_ref
  119.9 1.5 %other.1 = (bf16[448,512]{1,0:T(8,128)(2,1)}, bf16[448,512]{1,0:T(8,128)(2,1)}) custom-call(bf16[320,896]{1,0:T(8,128)(2,1)S(1)} %get-tuple-element.8.rows_ref, bf16[320,1024]{1,0:T(8,128)(2,1)S(1)} %collective-permute-done.1.other_ref, f32[512,1024]{1,0:T(8,128)S(1)} %own.1.total_ref), custom_call_target="tpu_custom_call" | custom-call | tf_op jit(solution)/shard_map/other/pallas_call | solution.py:293
Async XLA Ops:
  0.6 54.6 %copy-start.2 = (bf16[512,448]{0,1:T(8,128)(2,1)S(1)}, bf16[512,448]{0,1:T(8,128)(2,1)}, u32[]{:S(2)}) copy-start(bf16[512,448]{0,1:T(8,128)(2,1)} %param.13) | copy-start | bytes 1376260
  0.6 54.6 %copy-start.1 = (bf16[448,512]{1,0:T(8,128)(2,1)S(1)}, bf16[448,512]{1,0:T(8,128)(2,1)}, u32[]{:S(2)}) copy-start(bf16[448,512]{1,0:T(8,128)(2,1)} %refs_3_.1) | copy-start | bytes 1376260
  0.7 54.6 %copy-start = (bf16[448,512]{1,0:T(8,128)(2,1)S(1)}, bf16[448,512]{1,0:T(8,128)(2,1)}, u32[]{:S(2)}) copy-start(bf16[448,512]{1,0:T(8,128)(2,1)} %refs_2_.1) | copy-start | bytes 1376260
  56.7 5.3 %collective-permute-start = (bf16[320,1536]{1,0:T(8,128)(2,1)S(1)}, bf16[320,1536]{1,0:T(8,128)(2,1)S(1)}, u32[]{:S(2)}, u32[]{:S(2)}) collective-permute-start(bf16[320,1536]{1,0:T(8,128)(2,1)S(1)} %get-tuple-element.12), channel_id=1, source_target_pairs={{0,1},{1,0},{2,3},{3,2},{4,5},{5,4},{6,7},{7,6},{8,9},{9,8},{10,11... | collective-permute-start | bytes 2949128 | tf_op jit(solution)/shard_map/ppermute | solution.py:250
  112.3 7.6 %collective-permute-start.1 = (bf16[320,1024]{1,0:T(8,128)(2,1)S(1)}, bf16[320,1024]{1,0:T(8,128)(2,1)S(1)}, u32[]{:S(2)}, u32[]{:S(2)}) collective-permute-start(bf16[320,1024]{1,0:T(8,128)(2,1)S(1)} %bitcast.8), channel_id=1, source_target_pairs={{0,1},{1,0},{2,3},{3,2},{4,5},{5,4},{6,7},{7,6},{8,9},{9,8},{10,11... | collective-permute-start | bytes 1966088 | tf_op jit(solution)/shard_map/ppermute | solution.py:281

commit v4 on v3

--- a/solution.py
+++ b/solution.py
@@ -172,23 +172,29 @@
         out_ref[j, :, hidden:] = up_grad
 
 
-def outer(rows_ref, factor_ref, wide):
-    rows = rows_ref[:, rows_ref.shape[1] - wide :]
-    return lax.dot_general(
-        rows, factor_ref[...], (((0,), (0,)), ((), ())), preferred_element_type=F32
-    )
-
-
-def own_kernel(rows_ref, own_ref, total_ref):
-    total_ref[...] = outer(rows_ref, own_ref, total_ref.shape[0])
-
-
-def other_kernel(rows_ref, other_ref, total_ref, gate_ref, up_ref):
+def own_kernel(rows_ref, own_ref, other_rows_ref, total_ref, turned_ref):
+    wide = total_ref.shape[0]
+    left = rows_ref.shape[1] - wide
+    total_ref[...] = lax.dot_general(
+        rows_ref[:, left:], own_ref[...], (((0,), (0,)), ((), ())), preferred_element_type=F32
+    )
+    turned_ref[...] = other_rows_ref[:, left:].T
+
+
+def other_kernel(turned_ref, other_ref, total_ref, gate_hbm, up_hbm, gate_ref, up_ref, sems):
     wide = total_ref.shape[0]
     depth, hidden = gate_ref.shape
-    total = total_ref[...] + outer(rows_ref, other_ref, wide)
-    gate_ref[...] = total[wide - depth :, :hidden].astype(BF16)
-    up_ref[...] = total[wide - depth :, hidden:].astype(BF16)
+    copies = []
+    for i, (block_ref, out_hbm) in enumerate(((gate_ref, gate_hbm), (up_ref, up_hbm))):
+        here = slice(i * hidden, (i + 1) * hidden)
+        total = total_ref[:, here] + jnp.dot(
+            turned_ref[...], other_ref[:, here], preferred_element_type=F32
+        )
+        block_ref[...] = total[wide - depth :].astype(BF16)
+        copies.append(pltpu.make_async_copy(block_ref, out_hbm, sems.at[i]))
+        copies[-1].start()
+    for copy in copies:
+        copy.wait()
 
 
 def shards(tokens, routes, route_weight, out_grad, w_gate, w_up, w_down):
@@ -279,17 +285,20 @@
         spread, ("chip", "core"), split_axis=0, concat_axis=0, axis_index_groups=rings, tiled=True
     ).reshape(half, 2 * hidden)
     other = lax.ppermute(own, "core", pairs)
-    total = pl.pallas_call(
+    total, turned = pl.pallas_call(
         own_kernel,
-        out_shape=jax.ShapeDtypeStruct((wide, 2 * hidden), F32),
-        in_specs=whole(2),
-        out_specs=whole(1)[0],
+        out_shape=(
+            jax.ShapeDtypeStruct((wide, 2 * hidden), F32),
+            jax.ShapeDtypeStruct((wide, half), BF16),
+        ),
+        in_specs=whole(3),
+        out_specs=tuple(whole(2)),
         compiler_params=limit,
         cost_estimate=pl.CostEstimate(
             flops=4 * half * wide * hidden, bytes_accessed=8 << 20, transcendentals=0
         ),
         name="own",
-    )(own_rows, own)
+    )(own_rows, own, other_rows)
     return pl.pallas_call(
         other_kernel,
         out_shape=(
@@ -297,10 +306,15 @@
             jax.ShapeDtypeStruct((depth, hidden), BF16),
         ),
         in_specs=whole(3),
-        out_specs=tuple(whole(2)),
+        out_specs=tuple(apart(2)),
+        scratch_shapes=[
+            VMEM((depth, hidden), BF16),
+            VMEM((depth, hidden), BF16),
+            pltpu.SemaphoreType.DMA((2,)),
+        ],
         compiler_params=limit,
         name="other",
-    )(other_rows, other, total)
+    )(turned, other, total)
 
 
 def solution(mesh):

time: 123 us -> 123 us (level)
  no operation moved by 1% of the time
where the time goes in v4:
time: 123 us; the launch traced here: 121 us
  blocking collectives  102 us (83%)
  starting transfers between devices  8.98 us (7%)
  Pallas kernels  7.34 us (6%)
  waiting for transfers between devices  2.2 us (2%)
    all_to_all x1, blocking collectives, shards(): lax.all_to_all(blocks, ('expert', 'core'), split_axis=0, concat_axis=0, a...  52 us
    all_to_all x1, blocking collectives, shards(): lax.all_to_all(summed.reshape(chips, half // chips, 3 * hidden), ('chip',...  28.3 us
    all_to_all x1, blocking collectives, shards(): lax.all_to_all(spread, ('chip', 'core'), split_axis=0, concat_axis=0, axi...  21.6 us
    ppermute x1, starting transfers between devices, shards(): other = lax.ppermute(own, 'core', pairs)  5.85 us
    ppermute x1, starting transfers between devices, shards(): sibling = lax.ppermute(send, 'core', pairs)  3.13 us
    pallas_call x1, Pallas kernels, shards(): pl.pallas_call(lambda *refs: pack_kernel(capacity, *refs), out_shape=jax....  2.59 us
  transfers between devices with their start and end apart: 2, of which 2 were waited for; matrix products, arithmetic and copies ran while one was open for 0% of the time, Pallas kernels for 1%

profile of v4, /device:TPU:1, one launch (start us, length us, event | category | flops | bytes accessed | tf_op | source)
XLA Modules:
  0.0 121.4 jit_solution(14127215841763955189)
XLA Ops:
  0.6 0.0 copy-start.2
  0.6 0.0 copy-start.1
  0.7 0.0 copy-start
  0.7 2.6 %pack.1 = bf16[64,72,128]{2,1,0:T(8,128)(2,1)} custom-call(s32[1]{0:T(128)} %bitcast.refs_0_, s32[1,128]{1,0:T(1,128)} %bitcast.14, bf16[1,128]{1,0:T(2,128)(2,1)} %bitcast.15, bf16[448,128]{1,0:T(8,128)(2,1)} %bitcast.12, bf16[448,128]{1,0:T(8,128)(2,1)} %bitcast.13), custom_call_target="tpu_custom_call" | custom-call | tf_op jit(solution)/shard_map/pack/pallas_call | solution.py:224
  3.3 52.0 %all_to_all.15.refs_1_ = bf16[64,72,128]{2,1,0:T(8,128)(2,1)S(1)} all-to-all(bf16[64,72,128]{2,1,0:T(8,128)(2,1)} %pack.1), channel_id=1, replica_groups={{0,16,32,48,64,80,96,112,128,144,160,176,192,208,224,240,256,272,288,30..., dimensions={0} | all-to-all | bytes 2359296 | tf_op jit(solution)/shard_map/all_to_all | solution.py:239
  55.2 0.0 copy-done.2
  55.2 0.0 copy-done.1
  55.2 0.0 copy-done
  55.2 1.4 %send.1 = (bf16[320,896]{1,0:T(8,128)(2,1)S(1)}, bf16[320,1536]{1,0:T(8,128)(2,1)S(1)}, bf16[512,1024]{1,0:T(8,128)(2,1)S(1)}, bf16[512,512]{1,0:T(8,128)(2,1)S(1)}) custom-call(s32[1]{0:T(128)} %bitcast.refs_0_, bf16[64,72,128]{2,1,0:T(8,128)(2,1)S(1)} %all_to_all.15.refs_1_, bf16[448,512]{1,0:T(8,128)(2,1)S(1)} %copy-done, bf16[448,512]{1,0:T(8,128)(2,1)S(1)} %copy-done.1, ...), custom_call_target="tpu_custom_call" | custom-call | tf_op jit(solution)/shard_map/send/pallas_call | solution.py:242
  56.7 3.1 %collective-permute-start = (bf16[320,1536]{1,0:T(8,128)(2,1)S(1)}, bf16[320,1536]{1,0:T(8,128)(2,1)S(1)}, u32[]{:S(2)}, u32[]{:S(2)}) collective-permute-start(bf16[320,1536]{1,0:T(8,128)(2,1)S(1)} %get-tuple-element.14), channel_id=1, source_target_pairs={{0,1},{1,0},{2,3},{3,2},{4,5},{5,4},{6,7},{7,6},{8,9},{9,8},{10,11... | collective-permute-start | bytes 2949128 | tf_op jit(solution)/shard_map/ppermute | solution.py:256
  59.8 0.9 keep.1
  60.7 1.2 %collective-permute-done = bf16[320,1536]{1,0:T(8,128)(2,1)S(1)} collective-permute-done((bf16[320,1536]{1,0:T(8,128)(2,1)S(1)}, bf16[320,1536]{1,0:T(8,128)(2,1)S(1)}, u32[]{:S(2)}, u32[]{:S(2)}) %collective-permute-start) | collective-permute-done | bytes 983072 | tf_op jit(solution)/shard_map/ppermute | solution.py:256
  62.0 0.2 add_convert_fusion
  62.2 28.3 %all_to_all.16.parts_ref = bf16[8,40,1536]{2,1,0:T(8,128)(2,1)S(1)} all-to-all(bf16[8,40,1536]{2,1,0:T(8,128)(2,1)S(1)} %bitcast.11), channel_id=1, replica_groups={{0,2,4,6,8,10,12,14},{15,13,11,9,7,5,3,1},{16,18,20,22,24,26,28,30},{31..., dimensions={0} | all-to-all | bytes 1966080 | tf_op jit(solution)/shard_map/all_to_all | solution.py:272
  90.5 0.2 factor.1
  90.7 21.6 %all_to_all.17 = bf16[8,40,1024]{2,1,0:T(8,128)(2,1)S(1)} all-to-all(bf16[8,40,1024]{2,1,0:T(8,128)(2,1)S(1)} %factor.1), channel_id=1, replica_groups={{0,2,4,6,8,10,12,14},{15,13,11,9,7,5,3,1},{16,18,20,22,24,26,28,30},{31..., dimensions={0} | all-to-all | bytes 1310720 | tf_op jit(solution)/shard_map/all_to_all | solution.py:284
  112.3 5.9 %collective-permute-start.1 = (bf16[320,1024]{1,0:T(8,128)(2,1)S(1)}, bf16[320,1024]{1,0:T(8,128)(2,1)S(1)}, u32[]{:S(2)}, u32[]{:S(2)}) collective-permute-start(bf16[320,1024]{1,0:T(8,128)(2,1)S(1)} %bitcast.8), channel_id=1, source_target_pairs={{0,1},{1,0},{2,3},{3,2},{4,5},{5,4},{6,7},{7,6},{8,9},{9,8},{10,11... | collective-permute-start | bytes 1966088 | tf_op jit(solution)/shard_map/ppermute | solution.py:287
  118.2 0.7 own.1
  118.9 1.0 collective-permute-done.1.other_ref
  119.9 1.5 %other.1 = (bf16[448,512]{1,0:T(8,128)(2,1)}, bf16[448,512]{1,0:T(8,128)(2,1)}) custom-call(bf16[512,320]{1,0:T(8,128)(2,1)S(1)} %get-tuple-element.16.turned_ref, bf16[320,1024]{1,0:T(8,128)(2,1)S(1)} %collective-permute-done.1.other_ref, f32[512,1024]{1,0:T(8,128)S(1)} %get-tuple-element.17.total_ref), custom_call_target="tpu_custom_call" | custom-call | tf_op jit(solution)/shard_map/other/pallas_call | solution.py:302
Async XLA Ops:
  0.6 54.6 %copy-start.2 = (bf16[512,448]{0,1:T(8,128)(2,1)S(1)}, bf16[512,448]{0,1:T(8,128)(2,1)}, u32[]{:S(2)}) copy-start(bf16[512,448]{0,1:T(8,128)(2,1)} %param.13) | copy-start | bytes 1376260
  0.6 54.6 %copy-start.1 = (bf16[448,512]{1,0:T(8,128)(2,1)S(1)}, bf16[448,512]{1,0:T(8,128)(2,1)}, u32[]{:S(2)}) copy-start(bf16[448,512]{1,0:T(8,128)(2,1)} %refs_3_.1) | copy-start | bytes 1376260
  0.7 54.6 %copy-start = (bf16[448,512]{1,0:T(8,128)(2,1)S(1)}, bf16[448,512]{1,0:T(8,128)(2,1)}, u32[]{:S(2)}) copy-start(bf16[448,512]{1,0:T(8,128)(2,1)} %refs_2_.1) | copy-start | bytes 1376260
  56.7 5.3 %collective-permute-start = (bf16[320,1536]{1,0:T(8,128)(2,1)S(1)}, bf16[320,1536]{1,0:T(8,128)(2,1)S(1)}, u32[]{:S(2)}, u32[]{:S(2)}) collective-permute-start(bf16[320,1536]{1,0:T(8,128)(2,1)S(1)} %get-tuple-element.14), channel_id=1, source_target_pairs={{0,1},{1,0},{2,3},{3,2},{4,5},{5,4},{6,7},{7,6},{8,9},{9,8},{10,11... | collective-permute-start | bytes 2949128 | tf_op jit(solution)/shard_map/ppermute | solution.py:256
  112.3 7.6 %collective-permute-start.1 = (bf16[320,1024]{1,0:T(8,128)(2,1)S(1)}, bf16[320,1024]{1,0:T(8,128)(2,1)S(1)}, u32[]{:S(2)}, u32[]{:S(2)}) collective-permute-start(bf16[320,1024]{1,0:T(8,128)(2,1)S(1)} %bitcast.8), channel_id=1, source_target_pairs={{0,1},{1,0},{2,3},{3,2},{4,5},{5,4},{6,7},{7,6},{8,9},{9,8},{10,11... | collective-permute-start | bytes 1966088 | tf_op jit(solution)/shard_map/ppermute | solution.py:287
